TPU v7x, 256 devices: a whole 4x4x8 slice. The times are simulated.
256 devices in a mesh: ev: 4 (over z_hi, core), st: 64 (over x, z_lo, y).
Axes of the slice: x: 4, y: 4, z: 8 (z_hi: 2, z_lo: 4; z = z_hi * 4 + z_lo), core: 2. Of those that a mesh axis runs over, the one named last changes fastest.
Arguments:
- waveforms: bfloat16 [192, 512, 384], P('st', 'ev'), may hold values from -160 to 160
- availability: int32 [192, 512], P('st', 'ev'), may hold values 0 or 1
- lag_offset: int32 [192], P('st'), may hold values from -4 to 4
Outputs:
- correlation: float32 [17, 512, 512], P(None, ('ev', 'st'))
All inputs are finite; a program needn't handle non-finite values. No bound on the sum of `availability` on one device may be relied on, other than what follows from the above.
Results may differ from a plain program's by a relative error of at most 0.0024.
Values may be sent and summed in bfloat16 or wider, within the bound.
A program may use at most 128 MiB of HBM per device.

v0:
```python
import jax
import jax.numpy as jnp
from jax import lax
from jax.sharding import PartitionSpec as P

LAGS = 17
SHIFT_MOST = 4
epsilon = 1e-06


def normalize(waveforms, availability):
    wave_float = waveforms.astype(jnp.float32)
    energy = jnp.sum(wave_float * wave_float, axis=-1, keepdims=True)
    inverse_norm = availability.astype(jnp.float32)[..., None] * lax.rsqrt(energy + epsilon)
    return (wave_float * inverse_norm).astype(jnp.bfloat16)


def lag_stack(other_rows, shift_now):
    rows_other = other_rows.shape[0]
    samples = other_rows.shape[1] // 3
    pad_reach = SHIFT_MOST + (LAGS - 1) // 2
    split_rows = other_rows.reshape(rows_other, 3, samples)
    padded = jnp.pad(split_rows, ((0, 0), (0, 0), (pad_reach, pad_reach)))
    window = lax.dynamic_slice_in_dim(padded, SHIFT_MOST + shift_now, samples + LAGS - 1, 2)
    shifted = jnp.stack(
        [window[:, :, lag_index : lag_index + samples] for lag_index in range(LAGS)], 0
    )
    return shifted.reshape(LAGS, rows_other, 3 * samples)


def station_terms(own_block, other_block, offsets):
    shifted = jax.vmap(lag_stack)(other_block, offsets)
    return jnp.einsum("sik,sljk->lij", own_block, shifted, preferred_element_type=jnp.float32)


def on_device(waveforms, availability, lag_offset):
    unit_waves = normalize(waveforms, availability)
    ev_count = lax.axis_size("ev")
    ev_rows = unit_waves.shape[1]
    columns = ev_rows * ev_count
    gathered = lax.all_gather(unit_waves, "ev", axis=1, tiled=True)
    blocks = [
        (gathered[:, member * ev_rows : (member + 1) * ev_rows], jnp.int32(member * ev_rows))
        for member in range(ev_count)
    ]
    totals = jnp.zeros((LAGS, ev_rows, columns), jnp.float32)
    for other_block, first_col in blocks:
        partial_value = station_terms(unit_waves, other_block, lag_offset)
        totals = lax.dynamic_update_slice(totals, partial_value, (0, 0, first_col))
    return lax.psum_scatter(totals, "st", scatter_dimension=1, tiled=True)


def solution(mesh):
    placed = (P("st", "ev", None), P("st", "ev"), P("st"))
    return jax.shard_map(
        on_device,
        mesh=mesh,
        in_specs=placed,
        out_specs=P(None, ("ev", "st"), None),
        check_vma=False,
    )
```

profile of v0, /device:TPU:0, one launch (start us, length us, event | category | flops | bytes accessed | tf_op | source)
XLA Modules:
  0.0 487.4 jit_solution(12378270814222042738)
XLA Ops:
  6.5 1.2 copy.27
  7.8 0.7 rsqrt_multiply_fusion
  8.5 0.8 fusion.4
  9.3 0.7 fusion.78
  10.0 34.0 %all-gather.2.cloned.1.call-done = bf16[3,512,384]{1,2,0:T(8,128)(2,1)} async-done(((bf16[3,128,384]{1,2,0:T(8,128)(2,1)}), bf16[3,512,384]{1,2,0:T(8,128)(2,1)}) %all-gather.2.cloned.1.call-update) | async-done | bytes 1179664 | tf_op jit(solution)/shard_map/all_gather | solution.py:41
  44.0 1.3 fusion.79
  45.3 0.3 copy.28
  45.7 1.2 gather_fusion
  47.0 0.2 fusion.71
  47.4 0.2 fusion.69
  47.6 0.2 fusion.68
  47.7 0.2 fusion.67
  47.9 0.2 fusion.66
  48.1 0.2 fusion.65
  48.3 0.2 fusion.64
  48.4 0.2 fusion.63
  49.5 0.2 fusion.57
  49.8 1.5 copy.29
  51.3 1.5 convolution_bitcast_fusion.3
  52.8 0.3 copy.32
  53.3 1.2 gather_fusion.1
  54.6 0.2 fusion.54
  54.9 0.2 fusion.52
  55.1 0.2 fusion.51
  55.3 0.2 fusion.50
  55.5 0.2 fusion.49
  55.6 0.2 fusion.48
  55.8 0.2 fusion.47
  56.0 0.2 fusion.46
  56.3 0.2 fusion.44
  56.5 0.2 fusion.43
  57.0 0.2 fusion.40
  57.4 3.7 copy.33
  61.0 0.3 copy.36
  61.5 1.3 gather_fusion.2
  63.0 0.2 fusion.37
  63.3 0.2 fusion.35
  63.5 0.2 fusion.34
  63.7 0.2 fusion.33
  63.8 0.2 fusion.32
  64.0 0.2 fusion.31
  64.2 0.2 fusion.30
  64.4 0.2 fusion.29
  65.4 0.2 fusion.23
  65.7 3.8 copy.37
  69.5 0.3 copy.40
  69.9 1.2 gather_fusion.3
  71.2 0.2 fusion.20
  71.6 0.2 fusion.18
  71.8 0.2 fusion.17
  71.9 0.2 fusion.16
  72.1 0.2 fusion.15
  72.3 0.2 fusion.14
  72.5 0.2 fusion.13
  72.6 0.2 fusion.12
  74.0 3.4 copy-done.1
  77.4 4.5 copy.41
  82.0 2.5 dynamic_update_slice.12
  84.4 2.6 fusion.2
  87.0 2.8 fusion.1
  89.8 2.5 fusion
  92.3 6.2 %copy.44 = f32[17,128,512]{2,0,1:T(8,128)} copy(f32[17,128,512]{1,2,0:T(8,128)} %fusion) | data formatting | bytes 8912896 | tf_op jit(solution)/shard_map/dynamic_update_slice | solution.py:49
  98.6 380.4 %reduce-scatter.2.cloned.1.call-done = f32[17,2,512]{2,0,1:T(8,128)} async-done(((f32[17,128,512]{2,0,1:T(8,128)}), f32[17,2,512]{2,0,1:T(8,128)}) %reduce-scatter.2.cloned.1.call-update) | async-done | bytes 69648 | tf_op jit(solution)/shard_map/reduce_scatter | solution.py:50
  479.0 1.6 copy.45
  (53 shorter events, 6.0 us)
Async XLA Ops:
  6.5 37.4 %all-gather.2.cloned.1.call-start = ((), (), s32[]{:S(2)}) async-start(), calls=%async_computation.1 | async-start | bytes 1474560 | tf_op jit(solution)/shard_map/all_gather | solution.py:41
  9.3 469.7 %reduce-scatter.2.cloned.1.call-start = ((), (), s32[]{:S(2)}) async-start(), calls=%async_computation.2 | async-start | bytes 6389760 | tf_op jit(solution)/shard_map/reduce_scatter | solution.py:50
  49.5 1.8 copy-start
  73.9 10.6 %slice-start = ((s8[5013504]{0:T(1024)(128)(4,1)}), s8[4194304]{0:T(1024)(128)(4,1)S(1)}, s32[]{:S(2)}) async-start(s8[5013504]{0:T(1024)(128)(4,1)} %bitcast.330), calls=%async_computation.3 | async-start | bytes 8388608
  74.0 3.4 copy-start.1
  77.4 7.0 %slice-start.1 = ((s8[5013504]{0:T(1024)(128)(4,1)}), s8[819200]{0:T(1024)(128)(4,1)S(1)}, s32[]{:S(2)}) async-start(s8[5013504]{0:T(1024)(128)(4,1)} %bitcast.330), calls=%async_computation.4 | async-start | bytes 1638400
  77.4 9.6 %slice-start.2 = ((s8[5013504]{0:T(1024)(128)(4,1)}), s8[4194304]{0:T(1024)(128)(4,1)S(1)}, s32[]{:S(2)}) async-start(s8[5013504]{0:T(1024)(128)(4,1)} %bitcast.333), calls=%async_computation.5 | async-start | bytes 8388608
  81.9 5.1 %slice-start.3 = ((s8[5013504]{0:T(1024)(128)(4,1)}), s8[819200]{0:T(1024)(128)(4,1)S(1)}, s32[]{:S(2)}) async-start(s8[5013504]{0:T(1024)(128)(4,1)} %bitcast.333), calls=%async_computation.6 | async-start | bytes 1638400
Sparse Core Ops, SparseCore 0:
  9.4 34.5 all-gather.1
  98.7 380.2 reduce-scatter.1
where the time goes:
time: 488 us; the launch traced here: 487 us
  waiting for transfers between devices  414 us (85%)
  local copies, waits for them, and re-layouts  47.7 us (10%)
  between operations  13.6 us (3%)
  matrix products  9.43 us (2%)
    reduce_scatter x1, waiting for transfers between devices, on_device(): return lax.psum_scatter(totals, 'st', scatter_dimension=1, tiled=True)  380 us
    all_gather x1, waiting for transfers between devices, on_device(): gathered = lax.all_gather(unit_waves, 'ev', axis=1, tiled=True)  34 us
    unnamed x77, local copies, waits for them, and re-layouts  15.5 us
    transpose x4, local copies, waits for them, and re-layouts, lag_stack(): return shifted.reshape(LAGS, rows_other, 3 * samples)  13.4 us
  transfers between devices with their start and end apart: 2, of which 2 were waited for; matrix products, arithmetic and copies ran while one was open for 0% of the time, Pallas kernels for 0%

commit v1 on v0

--- a/solution.py
+++ b/solution.py
@@ -38,7 +38,9 @@
     ev_count = lax.axis_size("ev")
     ev_rows = unit_waves.shape[1]
     columns = ev_rows * ev_count
-    gathered = lax.all_gather(unit_waves, "ev", axis=1, tiled=True)
+    gathered = jnp.concatenate(
+        lax.all_to_all(jnp.stack([unit_waves] * lax.axis_size("ev")), "ev", 0, 0), axis=1
+    )
     blocks = [
         (gathered[:, member * ev_rows : (member + 1) * ev_rows], jnp.int32(member * ev_rows))
         for member in range(ev_count)

time: 488 us -> 494 us (1.012)
  starting transfers between devices: 0.04 us -> 6.72 us
    all_gather x1 -> x0, waiting for transfers between devices: 34 us -> none  [on_device(): gathered = lax.all_gather(unit_waves, 'ev', axis=1, tiled=True)]
    all_to_all x0 -> x1, waiting for transfers between devices: none -> 30.9 us  [on_device(): lax.all_to_all(jnp.stack([unit_waves] * lax.axis_size('ev')), 'ev', 0, 0)]
    all_to_all x0 -> x1, starting transfers between devices: none -> 6.72 us  [on_device(): lax.all_to_all(jnp.stack([unit_waves] * lax.axis_size('ev')), 'ev', 0, 0)]
    unnamed x77 -> x74, local copies, waits for them, and re-layouts: 15.5 us -> 14.4 us
where the time goes in v1:
time: 494 us
  waiting for transfers between devices  413 us (84%)
  local copies, waits for them, and re-layouts  47.5 us (10%)
  between operations  13.6 us (3%)
  matrix products  9.36 us (2%)
  starting transfers between devices  6.72 us (1%)
    reduce_scatter x1, waiting for transfers between devices, on_device(): return lax.psum_scatter(totals, 'st', scatter_dimension=1, tiled=True)  382 us
    all_to_all x1, waiting for transfers between devices, on_device(): lax.all_to_all(jnp.stack([unit_waves] * lax.axis_size('ev')), 'ev', 0, 0)  30.9 us
    unnamed x74, local copies, waits for them, and re-layouts  14.4 us
    transpose x4, local copies, waits for them, and re-layouts, lag_stack(): return shifted.reshape(LAGS, rows_other, 3 * samples)  13.4 us
  transfers between devices with their start and end apart: 2, of which 2 were waited for; matrix products, arithmetic and copies ran while one was open for 0% of the time, Pallas kernels for 0%

profile of v1, /device:TPU:0, one launch (start us, length us, event | category | flops | bytes accessed | tf_op | source)
XLA Modules:
  0.0 494.0 jit_solution(3484445403509683217)
XLA Ops:
  6.5 1.1 fusion.3
  7.6 0.7 rsqrt_multiply_fusion
  8.3 1.1 fusion.4
  9.4 1.2 stack.223
  10.6 6.7 %all-to-all-start = ((bf16[4,3,128,384]{3,2,1,0:T(8,128)(2,1)}), bf16[4,3,128,384]{3,2,1,0:T(8,128)(2,1)S(1)}, u32[]{:S(2)}, u32[]{:S(2)}) async-start(bf16[4,3,128,384]{3,2,1,0:T(8,128)(2,1)} %stack.223), calls=%async_computation | async-start | bytes 2359296 | tf_op jit(solution)/shard_map/all_to_all | solution.py:42
  17.3 0.7 fusion.78
  18.0 30.9 %all-to-all-done = bf16[4,3,128,384]{3,2,1,0:T(8,128)(2,1)S(1)} async-done(((bf16[4,3,128,384]{3,2,1,0:T(8,128)(2,1)}), bf16[4,3,128,384]{3,2,1,0:T(8,128)(2,1)S(1)}, u32[]{:S(2)}, u32[]{:S(2)}) %all-to-all-start) | async-done | bytes 1179680 | tf_op jit(solution)/shard_map/all_to_all | solution.py:42
  49.1 0.2 copy.27
  49.4 0.3 copy.28
  49.8 1.2 gather_fusion
  51.1 0.2 fusion.71
  51.4 0.2 fusion.69
  51.6 0.2 fusion.68
  51.8 0.2 fusion.67
  52.0 0.2 fusion.66
  52.2 0.2 fusion.65
  52.3 0.2 fusion.64
  52.5 0.2 fusion.63
  53.9 1.5 copy.29
  55.3 1.5 convolution_bitcast_fusion.3
  56.9 0.2 copy.31
  57.1 0.3 copy.32
  57.5 1.2 gather_fusion.1
  58.9 0.2 fusion.54
  59.2 0.2 fusion.52
  59.4 0.2 fusion.51
  59.5 0.2 fusion.50
  59.7 0.2 fusion.49
  59.9 0.2 fusion.48
  60.1 0.2 fusion.47
  60.3 0.2 fusion.46
  61.6 3.7 copy.33
  65.3 0.2 copy.35
  65.5 0.4 copy.36
  66.1 1.2 gather_fusion.2
  67.4 0.2 fusion.37
  67.8 0.2 fusion.35
  68.0 0.2 fusion.34
  68.1 0.2 fusion.33
  68.3 0.2 fusion.32
  68.5 0.2 fusion.31
  68.7 0.2 fusion.30
  68.8 0.2 fusion.29
  70.2 3.8 copy.37
  74.0 0.2 copy.39
  74.2 0.3 copy.40
  74.7 1.2 gather_fusion.3
  76.0 0.2 fusion.20
  76.3 0.2 fusion.18
  76.5 0.2 fusion.17
  76.7 0.2 fusion.16
  76.8 0.2 fusion.15
  77.0 0.2 fusion.14
  77.2 0.2 fusion.13
  77.4 0.2 fusion.12
  78.8 3.4 copy-done
  82.2 4.5 copy.41
  86.7 2.5 dynamic_update_slice.12
  89.2 2.5 fusion.2
  91.7 2.7 fusion.1
  94.4 2.5 fusion
  97.0 6.2 %copy.43 = f32[17,128,512]{2,0,1:T(8,128)} copy(f32[17,128,512]{1,2,0:T(8,128)} %fusion) | data formatting | bytes 8912896 | tf_op jit(solution)/shard_map/dynamic_update_slice | solution.py:51
  103.2 382.3 %reduce-scatter.2.cloned.1.call-done = f32[17,2,512]{2,0,1:T(8,128)} async-done(((f32[17,128,512]{2,0,1:T(8,128)}), f32[17,2,512]{2,0,1:T(8,128)}) %reduce-scatter.2.cloned.1.call-update) | async-done | bytes 69648 | tf_op jit(solution)/shard_map/reduce_scatter | solution.py:52
  485.6 1.6 copy.44
  (55 shorter events, 7.0 us)
Async XLA Ops:
  10.6 38.3 %all-to-all-start = ((bf16[4,3,128,384]{3,2,1,0:T(8,128)(2,1)}), bf16[4,3,128,384]{3,2,1,0:T(8,128)(2,1)S(1)}, u32[]{:S(2)}, u32[]{:S(2)}) async-start(bf16[4,3,128,384]{3,2,1,0:T(8,128)(2,1)} %stack.223), calls=%async_computation | async-start | bytes 2359296 | tf_op jit(solution)/shard_map/all_to_all | solution.py:42
  17.3 468.3 %reduce-scatter.2.cloned.1.call-start = ((), (), s32[]{:S(2)}) async-start(), calls=%async_computation.2 | async-start | bytes 6389760 | tf_op jit(solution)/shard_map/reduce_scatter | solution.py:52
  78.6 10.6 %slice-start = ((s8[5013504]{0:T(1024)(128)(4,1)}), s8[4194304]{0:T(1024)(128)(4,1)S(1)}, s32[]{:S(2)}) async-start(s8[5013504]{0:T(1024)(128)(4,1)} %bitcast.330), calls=%async_computation.3 | async-start | bytes 8388608
  78.8 3.4 copy-start
  82.1 7.0 %slice-start.1 = ((s8[5013504]{0:T(1024)(128)(4,1)}), s8[819200]{0:T(1024)(128)(4,1)S(1)}, s32[]{:S(2)}) async-start(s8[5013504]{0:T(1024)(128)(4,1)} %bitcast.330), calls=%async_computation.4 | async-start | bytes 1638400
  82.1 9.5 %slice-start.2 = ((s8[5013504]{0:T(1024)(128)(4,1)}), s8[4194304]{0:T(1024)(128)(4,1)S(1)}, s32[]{:S(2)}) async-start(s8[5013504]{0:T(1024)(128)(4,1)} %bitcast.333), calls=%async_computation.5 | async-start | bytes 8388608
  86.7 5.0 %slice-start.3 = ((s8[5013504]{0:T(1024)(128)(4,1)}), s8[819200]{0:T(1024)(128)(4,1)S(1)}, s32[]{:S(2)}) async-start(s8[5013504]{0:T(1024)(128)(4,1)} %bitcast.333), calls=%async_computation.6 | async-start | bytes 1638400
Sparse Core Ops, SparseCore 0:
  103.4 382.1 reduce-scatter.1
